TPU v7x, 128 devices: a whole 4x4x4 slice. The times are simulated.
128 devices in a mesh: rep: 2 (over core), exp: 64 (over y, x, z).
Axes of the slice: x: 4, y: 4, z: 4, core: 2. Of those that a mesh axis runs over, the one named last changes fastest.
Arguments:
- tokens: bfloat16 [16384, 1024], P(('rep', 'exp')), may hold values from -6 to 6
- hash_ids: int32 [16384, 1], P(('rep', 'exp')), may hold values from 0 to 63; in each aligned block of 128 rows (0 to 127, 128 to 255, ...) at most 8 rows name the same one
- doc_lengths: int32 [128, 4], P(('rep', 'exp')), may hold values from 1 to 64, 128 in all within a row
- w_query: bfloat16 [1024, 1024], P(('rep', 'exp')), may hold values from -0.1875 to 0.1875
- w_key: bfloat16 [1024, 1024], P(('rep', 'exp')), may hold values from -0.1875 to 0.1875
- w_value: bfloat16 [1024, 1024], P(('rep', 'exp')), may hold values from -0.1875 to 0.1875
- w_output: bfloat16 [1024, 1024], P(('rep', 'exp')), may hold values from -0.5 to 0.5
- norm1_gain: bfloat16 [1024], P(('rep', 'exp')), may hold values from 0.5 to 1.5
- norm1_bias: bfloat16 [1024], P(('rep', 'exp')), may hold values from -1 to 1
- norm2_gain: bfloat16 [1024], P(('rep', 'exp')), may hold values from 0.5 to 1.5
- norm2_bias: bfloat16 [1024], P(('rep', 'exp')), may hold values from -1 to 1
- expert_in: bfloat16 [64, 1024, 4096], P('exp', None, 'rep'), may hold values from -0.1875 to 0.1875
- expert_out: bfloat16 [64, 4096, 1024], P('exp', 'rep'), may hold values from -0.09375 to 0.09375
- load_average: float32 [64], replicated, may hold values from 64 to 1024
- out_grad: bfloat16 [16384, 1024], P(('rep', 'exp')), may hold values from -6 to 6
Outputs:
- output: bfloat16 [16384, 1024], P(('rep', 'exp'))
- input_grad: float32 [16384, 1024], P(('rep', 'exp'))
- w_query_grad: float32 [1024, 1024], P(('rep', 'exp'))
- w_key_grad: float32 [1024, 1024], P(('rep', 'exp'))
- w_value_grad: float32 [1024, 1024], P(('rep', 'exp'))
- w_output_grad: float32 [1024, 1024], P(('rep', 'exp'))
- norm1_gain_grad: float32 [1024], P(('rep', 'exp'))
- norm1_bias_grad: float32 [1024], P(('rep', 'exp'))
- norm2_gain_grad: float32 [1024], P(('rep', 'exp'))
- norm2_bias_grad: float32 [1024], P(('rep', 'exp'))
- expert_in_grad: float32 [64, 1024, 4096], P('exp', None, 'rep')
- expert_out_grad: float32 [64, 4096, 1024], P('exp', 'rep')
- counts: int32 [64], replicated
- new_average: float32 [64], replicated
Inputs may be any that keep to these rules, and one draw needn't show every extreme that they name: `hash_ids`: in each aligned block of 128 rows (one device's tokens) no expert is named by more than 8 rows, a bound that some block reaches. `doc_lengths`: each row sums to 128; its largest entry is exactly 64.
All inputs are finite; a program needn't handle non-finite values.
Results may differ from a plain program's by a relative error of at most 0.012.
Values may be sent and summed in bfloat16 or wider, within the bound.
No kernel may reach another device: no remote copies, remote signals or barrier semaphores. Data moves between devices by JAX's collectives and lax.ppermute only.
A program may use at most 192 MiB of HBM per device.

v0:
```python
import jax
import jax.numpy as jnp
from jax import lax
from jax.sharding import PartitionSpec as P

HEADS = 16
HEAD_DIM = 64


EPSILON = 1e-05


def layer_norm(values, gain, shift):
    center = values - jnp.mean(values, axis=-1, keepdims=True)
    spread = jnp.mean(center * center, axis=-1, keepdims=True)
    return center * lax.rsqrt(spread + EPSILON) * gain + shift


def norm_backward(values, gain, shift, upstream):
    _, norm_pull = jax.vjp(layer_norm, values, gain, shift)
    return norm_pull(upstream)


def gelu_backward(pre, upstream):
    _, gelu_pull = jax.vjp(jax.nn.gelu, pre)
    return gelu_pull(upstream)[0]


def per_device(
    tokens,
    hash_ids,
    doc_lengths,
    w_query,
    w_key,
    w_value,
    w_output,
    norm1_gain,
    norm1_bias,
    norm2_gain,
    norm2_bias,
    expert_in,
    expert_out,
    load_average,
    out_grad,
):
    gathered = (
        lax.all_gather(w_query, ("rep", "exp"), axis=0, tiled=True),
        lax.all_gather(w_key, ("rep", "exp"), axis=0, tiled=True),
        lax.all_gather(w_value, ("rep", "exp"), axis=0, tiled=True),
        lax.all_gather(w_output, ("rep", "exp"), axis=0, tiled=True),
        lax.all_gather(norm1_gain, ("rep", "exp"), axis=0, tiled=True),
        lax.all_gather(norm1_bias, ("rep", "exp"), axis=0, tiled=True),
        lax.all_gather(norm2_gain, ("rep", "exp"), axis=0, tiled=True),
        lax.all_gather(norm2_bias, ("rep", "exp"), axis=0, tiled=True),
    )
    full_query, full_key, full_value, full_output = (
        gathered[0],
        gathered[1],
        gathered[2],
        gathered[3],
    )
    gain_one = gathered[4].astype(jnp.float32)
    bias_one = gathered[5].astype(jnp.float32)
    gain_two = gathered[6].astype(jnp.float32)
    bias_two = gathered[7].astype(jnp.float32)
    tok_count, width = tokens.shape
    scale = HEAD_DIM ** (-0.5)
    position = jnp.arange(tok_count, dtype=jnp.int32)
    ends = jnp.cumsum(doc_lengths[0])
    segment = jnp.sum((position[:, None] >= ends[None, :]).astype(jnp.int32), axis=1)
    allowed = (segment[:, None] == segment[None, :]) & (position[None, :] <= position[:, None])
    inputs = tokens.astype(jnp.float32)
    normed_low = layer_norm(inputs, gain_one, bias_one).astype(jnp.bfloat16)

    def project(weight):
        made = jnp.dot(normed_low, weight, preferred_element_type=jnp.float32).astype(jnp.bfloat16)
        return made.reshape(tok_count, HEADS, HEAD_DIM)

    queries = project(full_query)
    keys = project(full_key)
    values = project(full_value)

    def score_table():
        raw = jnp.einsum("qhd,khd->hqk", queries, keys, preferred_element_type=jnp.float32) * scale
        return jnp.where(allowed[None], raw, -1e30)

    scores = score_table()
    top_score = jnp.max(scores, axis=-1, keepdims=True)
    raised = jnp.exp(scores - top_score)
    total = jnp.sum(raised, axis=-1, keepdims=True)
    probs = raised / total
    log_total = top_score + jnp.log(total)
    attended = jnp.einsum(
        "hqk,khd->qhd", probs.astype(jnp.bfloat16), values, preferred_element_type=jnp.float32
    )
    attended = attended.astype(jnp.bfloat16).reshape(tok_count, width)
    branch = jnp.dot(attended, full_output, preferred_element_type=jnp.float32)
    hidden_one = inputs + branch
    normed_two_low = layer_norm(hidden_one, gain_two, bias_two).astype(jnp.bfloat16)
    experts_total = load_average.shape[0]
    capacity = max(2, 4 * tok_count // experts_total)
    groups = lax.axis_size("exp")
    local_experts = expert_in.shape[0]
    slot_rows = groups * capacity
    expert_ids = hash_ids[:, 0]
    choose = (expert_ids[:, None] == jnp.arange(experts_total, dtype=jnp.int32)[None, :]).astype(
        jnp.float32
    )
    earlier = (position[None, :] < position[:, None]).astype(jnp.float32)
    before = jnp.dot(earlier, choose, preferred_element_type=jnp.float32)
    rank = jnp.sum(before * choose, axis=1).astype(jnp.int32)
    slot = expert_ids * capacity + rank
    placing = (
        jnp.arange(experts_total * capacity, dtype=jnp.int32)[:, None] == slot[None, :]
    ).astype(jnp.bfloat16)
    counts = lax.psum(jnp.sum(choose, axis=0).astype(jnp.int32), ("rep", "exp"))
    new_average = 0.7 * load_average + 0.3 * counts.astype(jnp.float32)
    outgoing = jnp.dot(placing, normed_two_low, preferred_element_type=jnp.float32).astype(
        jnp.bfloat16
    )
    outgoing = outgoing.reshape(groups, local_experts, capacity, width)
    incoming = lax.all_to_all(outgoing, "exp", split_axis=0, concat_axis=2, tiled=True)
    expert_rows = incoming.reshape(local_experts, slot_rows, width)
    whole_in, whole_out = (
        lax.all_gather(expert_in, "rep", axis=2, tiled=True),
        lax.all_gather(expert_out, "rep", axis=1, tiled=True),
    )
    pre = jnp.einsum("erd,edf->erf", expert_rows, whole_in, preferred_element_type=jnp.float32)
    activated = jax.nn.gelu(pre).astype(jnp.bfloat16)
    result = jnp.einsum("erf,efd->erd", activated, whole_out, preferred_element_type=jnp.float32)
    result_low = result.astype(jnp.bfloat16).reshape(1, local_experts, slot_rows, width)
    returning = lax.all_to_all(result_low, "exp", split_axis=2, concat_axis=0, tiled=True)
    returning = returning.reshape(experts_total * capacity, width)
    expert_part = jnp.einsum("st,sd->td", placing, returning, preferred_element_type=jnp.float32)
    output = (hidden_one + expert_part).astype(jnp.bfloat16)
    upstream = out_grad.astype(jnp.float32)
    grad_slots = jnp.dot(placing, out_grad, preferred_element_type=jnp.float32).astype(jnp.bfloat16)
    grad_slots = grad_slots.reshape(groups, local_experts, capacity, width)
    grad_rows = lax.all_to_all(grad_slots, "exp", split_axis=0, concat_axis=2, tiled=True).reshape(
        local_experts, slot_rows, width
    )
    act_grad = jnp.einsum("erd,efd->erf", grad_rows, whole_out, preferred_element_type=jnp.float32)
    pre_grad = gelu_backward(pre, act_grad).astype(jnp.bfloat16)
    full_out_grad = jnp.einsum(
        "erf,erd->efd", activated, grad_rows, preferred_element_type=jnp.float32
    )
    full_in_grad = jnp.einsum(
        "erd,erf->edf", expert_rows, pre_grad, preferred_element_type=jnp.float32
    )
    in_weight_grad, out_weight_grad = (
        lax.psum_scatter(
            full_in_grad.astype(jnp.bfloat16), "rep", scatter_dimension=2, tiled=True
        ).astype(jnp.float32),
        lax.psum_scatter(
            full_out_grad.astype(jnp.bfloat16), "rep", scatter_dimension=1, tiled=True
        ).astype(jnp.float32),
    )
    rows_grad = jnp.einsum("erf,edf->erd", pre_grad, whole_in, preferred_element_type=jnp.float32)
    back_rows = rows_grad.astype(jnp.bfloat16).reshape(1, local_experts, slot_rows, width)
    back_slots = lax.all_to_all(back_rows, "exp", split_axis=2, concat_axis=0, tiled=True).reshape(
        experts_total * capacity, width
    )
    normed_two_grad = jnp.einsum(
        "st,sd->td", placing, back_slots, preferred_element_type=jnp.float32
    )
    hidden_part, gain_two_grad, bias_two_grad = norm_backward(
        hidden_one, gain_two, bias_two, normed_two_grad
    )
    hidden_grad = upstream + hidden_part
    branch_low = hidden_grad.astype(jnp.bfloat16)
    output_weight_grad = jnp.einsum(
        "td,te->de", attended, branch_low, preferred_element_type=jnp.float32
    )
    attended_grad = jnp.einsum(
        "te,de->td", branch_low, full_output, preferred_element_type=jnp.float32
    )
    attended_grad = attended_grad.astype(jnp.bfloat16).reshape(tok_count, HEADS, HEAD_DIM)
    again = jnp.exp(score_table() - log_total)
    probs_grad = jnp.einsum(
        "qhd,khd->hqk", attended_grad, values, preferred_element_type=jnp.float32
    )
    value_grad = jnp.einsum(
        "hqk,qhd->khd",
        again.astype(jnp.bfloat16),
        attended_grad,
        preferred_element_type=jnp.float32,
    ).astype(jnp.bfloat16)
    score_grad = again * (probs_grad - jnp.sum(again * probs_grad, axis=-1, keepdims=True))
    score_grad = score_grad.astype(jnp.bfloat16)
    query_grad = (
        jnp.einsum("hqk,khd->qhd", score_grad, keys, preferred_element_type=jnp.float32) * scale
    ).astype(jnp.bfloat16)
    key_grad = (
        jnp.einsum("hqk,qhd->khd", score_grad, queries, preferred_element_type=jnp.float32) * scale
    ).astype(jnp.bfloat16)
    query_flat = query_grad.reshape(tok_count, width)
    key_flat = key_grad.reshape(tok_count, width)
    value_flat = value_grad.reshape(tok_count, width)
    query_weight_grad = jnp.einsum(
        "td,te->de", normed_low, query_flat, preferred_element_type=jnp.float32
    )
    key_weight_grad = jnp.einsum(
        "td,te->de", normed_low, key_flat, preferred_element_type=jnp.float32
    )
    value_weight_grad = jnp.einsum(
        "td,te->de", normed_low, value_flat, preferred_element_type=jnp.float32
    )
    normed_one_grad = jnp.einsum(
        "te,de->td", query_flat, full_query, preferred_element_type=jnp.float32
    )
    normed_one_grad = normed_one_grad + jnp.einsum(
        "te,de->td", key_flat, full_key, preferred_element_type=jnp.float32
    )
    normed_one_grad = normed_one_grad + jnp.einsum(
        "te,de->td", value_flat, full_value, preferred_element_type=jnp.float32
    )
    input_part, gain_one_grad, bias_one_grad = norm_backward(
        inputs, gain_one, bias_one, normed_one_grad
    )
    input_grad = hidden_grad + input_part
    summed = (
        lax.psum_scatter(query_weight_grad, ("rep", "exp"), scatter_dimension=0, tiled=True),
        lax.psum_scatter(key_weight_grad, ("rep", "exp"), scatter_dimension=0, tiled=True),
        lax.psum_scatter(value_weight_grad, ("rep", "exp"), scatter_dimension=0, tiled=True),
        lax.psum_scatter(output_weight_grad, ("rep", "exp"), scatter_dimension=0, tiled=True),
        lax.psum_scatter(gain_one_grad, ("rep", "exp"), scatter_dimension=0, tiled=True),
        lax.psum_scatter(bias_one_grad, ("rep", "exp"), scatter_dimension=0, tiled=True),
        lax.psum_scatter(gain_two_grad, ("rep", "exp"), scatter_dimension=0, tiled=True),
        lax.psum_scatter(bias_two_grad, ("rep", "exp"), scatter_dimension=0, tiled=True),
    )
    return (
        output,
        input_grad,
        summed[0],
        summed[1],
        summed[2],
        summed[3],
        summed[4],
        summed[5],
        summed[6],
        summed[7],
        in_weight_grad,
        out_weight_grad,
        counts,
        new_average,
    )


def solution(mesh):
    return jax.shard_map(
        per_device,
        mesh=mesh,
        in_specs=(
            P(("rep", "exp"), None),
            P(("rep", "exp"), None),
            P(("rep", "exp"), None),
            P(("rep", "exp"), None),
            P(("rep", "exp"), None),
            P(("rep", "exp"), None),
            P(("rep", "exp"), None),
            P(("rep", "exp")),
            P(("rep", "exp")),
            P(("rep", "exp")),
            P(("rep", "exp")),
            P("exp", None, "rep"),
            P("exp", "rep", None),
            P(),
            P(("rep", "exp"), None),
        ),
        out_specs=(
            P(("rep", "exp"), None),
            P(("rep", "exp"), None),
            P(("rep", "exp"), None),
            P(("rep", "exp"), None),
            P(("rep", "exp"), None),
            P(("rep", "exp"), None),
            P(("rep", "exp")),
            P(("rep", "exp")),
            P(("rep", "exp")),
            P(("rep", "exp")),
            P("exp", None, "rep"),
            P("exp", "rep", None),
            P(),
            P(),
        ),
        check_vma=False,
    )
```

profile of v0, /device:TPU:1, one launch (start us, length us, event | category | flops | bytes accessed | tf_op | source)
XLA Modules:
  0.0 3079.9 jit_solution(13698509779164605813)
XLA Ops:
  12.2 69.7 %all-reduce.9 = (bf16[1024]{0:T(1024)(128)(2,1)S(1)}, bf16[1024]{0:T(1024)(128)(2,1)S(1)}, bf16[1024]{0:T(1024)(128)(2,1)S(1)}, bf16[1024]{0:T(1024)(128)(2,1)S(1)}) all-reduce(bf16[1024]{0:T(1024)(128)(2,1)S(1)} %dynamic-update-slice.1, bf16[1024]{0:T(1024)(128)(2,1)S(1)} %dynamic-update-slice, ...), channel_id=1, replica_groups=mesh['rep'=2,'exp'=64] {'rep','exp'}, use_global_device_ids=true, to_apply=%add.1 | all-reduce | flops 4096 | bytes 16384
  82.9 2.1 convolution_convert_fusion.7
  85.2 60.6 %all-gather.9.cloned.1.call-done = bf16[1024,1024]{1,0:T(8,128)(2,1)} async-done(((bf16[8,1024]{1,0:T(8,128)(2,1)}), bf16[1024,1024]{1,0:T(8,128)(2,1)}) %all-gather.9.cloned.1.call-update) | async-done | bytes 2097168 | tf_op jit(solution)/shard_map/all_gather | solution.py:47
  145.8 2.1 convolution_convert_fusion.6
  148.1 63.4 %all-gather.11.cloned.1.call-done = bf16[1024,1024]{1,0:T(8,128)(2,1)} async-done(((bf16[8,1024]{1,0:T(8,128)(2,1)}), bf16[1024,1024]{1,0:T(8,128)(2,1)}) %all-gather.11.cloned.1.call-update) | async-done | bytes 2097168 | tf_op jit(solution)/shard_map/all_gather | solution.py:48
  211.4 2.1 convolution_convert_fusion.5
  214.6 62.4 %all-gather.13.cloned.1.call-done = bf16[1024,1024]{1,0:T(8,128)(2,1)} async-done(((bf16[8,1024]{1,0:T(8,128)(2,1)}), bf16[1024,1024]{1,0:T(8,128)(2,1)}) %all-gather.13.cloned.1.call-update) | async-done | bytes 2097168 | tf_op jit(solution)/shard_map/all_gather | solution.py:50
  277.0 2.1 fusion.88
  280.9 6.2 all-to-all-start
  288.5 16.2 all-to-all-done
  305.7 4.8 all-to-all-start.2
  310.8 13.1 fusion.13
  324.0 2.9 all-to-all-done.2
  326.9 12.5 fusion.6
  339.4 2.0 copy-done.24
  341.5 6.8 convert_bitcast_fusion.1
  348.8 14.1 convert_bitcast_fusion
  362.9 10.7 fusion.24
  373.6 2.9 copy.103
  377.0 8.2 reduce.1
  385.3 1.5 reshape.329
  386.8 7.3 all-to-all-start.3
  394.2 16.3 all-to-all-done.3
  410.5 3.4 reshape.330
  413.9 2.2 multiply_reduce_fusion.1
  417.5 2.4 convolution_convert_fusion.3
  423.7 2.8 fusion.80
  427.7 2.8 fusion.78
  431.1 2.9 fusion.76
  434.1 2.6 fusion.90
  436.9 65.9 %psum.7 = s32[64]{0:T(128)S(1)} all-reduce(s32[64]{0:T(128)S(1)} %convert_element_type.176), channel_id=1, replica_groups=mesh['rep'=2,'exp'=64] {'rep','exp'}, use_global_device_ids=true, to_apply=%region_29.30 | all-reduce | flops 64 | bytes 512 | tf_op jit(solution)/shard_map/psum | solution.py:116
  503.3 10.9 fusion.21
  514.3 1.6 copy.104
  515.9 8.0 reduce
  523.9 2.6 reshape.327
  526.5 5.5 all-to-all-start.1
  532.0 2.5 fusion.89
  534.5 2.5 convolution_add_fusion.2
  537.1 3.3 fusion.85
  541.7 67.7 %all-reduce.8 = (f32[1024]{0:T(1024)S(1)}, f32[1024]{0:T(1024)S(1)}, f32[1024]{0:T(1024)S(1)}, f32[1024]{0:T(1024)S(1)}) all-reduce(f32[1024]{0:T(1024)S(1)} %get-tuple-element.16, f32[1024]{0:T(1024)S(1)} %get-tuple-element.19, f32[1024]{0:T(1024)S(1)} %get-tuple-element.14, ...), channel_id=6, replica_groups=mesh['rep'=2,'exp'=64] {'rep','exp'}, use_global_device_ids=true, to_apply=%region_19.20.clone | all-reduce | flops 4096 | bytes 32768
  611.7 6.5 reshape.328
  619.4 2.2 add_add_fusion.2
  621.6 6.7 convert_element_type.171
  628.3 6.7 convert_element_type.174
  634.9 447.5 %reduce-scatter.7.cloned.1.call-done = f32[8,1024]{1,0:T(8,128)} async-done(((f32[1024,1024]{1,0:T(8,128)}), f32[8,1024]{1,0:T(8,128)}) %reduce-scatter.7.cloned.1.call-update) | async-done | bytes 32784 | tf_op jit(solution)/shard_map/reduce_scatter | solution.py:222
  1082.5 666.5 %reduce-scatter.9.cloned.1.call-done = f32[8,1024]{1,0:T(8,128)} async-done(((f32[1024,1024]{1,0:T(8,128)}), f32[8,1024]{1,0:T(8,128)}) %reduce-scatter.9.cloned.1.call-update) | async-done | bytes 32784 | tf_op jit(solution)/shard_map/reduce_scatter | solution.py:223
  1749.0 661.8 %reduce-scatter.11.cloned.1.call-done = f32[8,1024]{1,0:T(8,128)} async-done(((f32[1024,1024]{1,0:T(8,128)}), f32[8,1024]{1,0:T(8,128)}) %reduce-scatter.11.cloned.1.call-update) | async-done | bytes 32784 | tf_op jit(solution)/shard_map/reduce_scatter | solution.py:224
  2410.8 661.8 %reduce-scatter.13.cloned.1.call-done = f32[8,1024]{1,0:T(8,128)} async-done(((f32[1024,1024]{1,0:T(8,128)}), f32[8,1024]{1,0:T(8,128)}) %reduce-scatter.13.cloned.1.call-update) | async-done | bytes 32784 | tf_op jit(solution)/shard_map/reduce_scatter | solution.py:225
  (134 shorter events, 25.0 us)
Async XLA Ops:
  7.2 4.0 copy-start.16
  7.2 4.3 copy-start.17
  7.2 4.5 copy-start.18
  7.2 4.7 copy-start.19
  7.2 74.7 %copy-start.20 = (s32[1,4]{1,0:T(1,128)S(1)}, s32[1,4]{1,0:T(1,128)}, u32[]{:S(2)}) copy-start(s32[1,4]{1,0:T(1,128)} %param.17) | copy-start | bytes 52
  7.2 74.9 %copy-start.21 = (s32[128,1]{0,1:T(1,128)S(1)}, s32[128,1]{0,1:T(1,128)}, u32[]{:S(2)}) copy-start(s32[128,1]{0,1:T(1,128)} %param.16) | copy-start | bytes 1540
  7.2 75.1 %copy-start = (bf16[128,1024]{1,0:T(8,128)(2,1)S(1)}, bf16[128,1024]{1,0:T(8,128)(2,1)}, u32[]{:S(2)}) copy-start(bf16[128,1024]{1,0:T(8,128)(2,1)} %param.15) | copy-start | bytes 786436
  7.2 75.6 %all-gather.7.cloned.1.call-start = ((), (), s32[]{:S(2)}) async-start(), calls=%async_computation.10 | async-start | bytes 2113536 | tf_op jit(solution)/shard_map/all_gather | solution.py:49
  8.0 137.8 %all-gather.9.cloned.1.call-start = ((), (), s32[]{:S(2)}) async-start(), calls=%async_computation.11 | async-start | bytes 2113536 | tf_op jit(solution)/shard_map/all_gather | solution.py:47
  8.7 202.7 %all-gather.11.cloned.1.call-start = ((), (), s32[]{:S(2)}) async-start(), calls=%async_computation.12 | async-start | bytes 2113536 | tf_op jit(solution)/shard_map/all_gather | solution.py:48
  9.5 267.5 %all-gather.13.cloned.1.call-start = ((), (), s32[]{:S(2)}) async-start(), calls=%async_computation.13 | async-start | bytes 2113536 | tf_op jit(solution)/shard_map/all_gather | solution.py:50
  10.0 300.8 %all-gather.15.cloned.1.call-start = ((), (), s32[]{:S(2)}) async-start(), calls=%async_computation.14 | async-start | bytes 12582912 | tf_op jit(solution)/shard_map/all_gather | solution.py:125
  10.6 316.3 %all-gather.17.cloned.1.call-start = ((), (), s32[]{:S(2)}) async-start(), calls=%async_computation.15 | async-start | bytes 12582912 | tf_op jit(solution)/shard_map/all_gather | solution.py:126
  85.2 194.2 %copy-start.11 = (bf16[128,1024]{0,1:T(8,128)(2,1)}, bf16[128,1024]{0,1:T(8,128)(2,1)S(1)}, u32[]{:S(2)}) copy-start(bf16[128,1024]{0,1:T(8,128)(2,1)S(1)} %copy.73) | copy-start | bytes 786436
  148.0 128.9 %copy-start.1 = (bf16[128,1024]{0,1:T(8,128)(2,1)}, bf16[128,1024]{0,1:T(8,128)(2,1)S(1)}, u32[]{:S(2)}) copy-start(bf16[128,1024]{0,1:T(8,128)(2,1)S(1)} %copy.74) | copy-start | bytes 786436
  148.0 139.0 %copy-start.6 = (bf16[128,1024]{1,0:T(8,128)(2,1)S(1)}, bf16[128,1024]{1,0:T(8,128)(2,1)}, u32[]{:S(2)}) copy-start(bf16[128,1024]{1,0:T(8,128)(2,1)} %param.29) | copy-start | bytes 786436
  213.7 63.3 %copy-start.3 = (bf16[128,1024]{0,1:T(8,128)(2,1)}, bf16[128,1024]{0,1:T(8,128)(2,1)S(1)}, u32[]{:S(2)}) copy-start(bf16[128,1024]{0,1:T(8,128)(2,1)S(1)} %copy.75) | copy-start | bytes 786436
  214.6 66.3 %copy-start.14 = (bf16[16,64,128]{2,1,0:T(8,128)(2,1)}, bf16[16,64,128]{2,1,0:T(8,128)(2,1)S(1)}, u32[]{:S(2)}) copy-start(bf16[16,64,128]{2,1,0:T(8,128)(2,1)S(1)} %convolution_convert_fusion.4) | copy-start | bytes 786436
  280.9 23.9 all-to-all-start
  304.8 1.0 copy-start.12
  305.7 21.2 all-to-all-start.2
  310.5 311.1 %reduce-scatter.15.cloned.1.call-start = ((), (), s32[]{:S(2)}) async-start(), calls=%async_computation.20 | async-start | bytes 12582912 | tf_op jit(solution)/shard_map/reduce_scatter | solution.py:151
  326.9 14.6 copy-start.13
  339.4 2.0 copy-start.24
  348.3 280.0 %reduce-scatter.17.cloned.1.call-start = ((), (), s32[]{:S(2)}) async-start(), calls=%async_computation.21 | async-start | bytes 12582912 | tf_op jit(solution)/shard_map/reduce_scatter | solution.py:154
  386.8 23.7 all-to-all-start.3
  394.1 688.4 %reduce-scatter.7.cloned.1.call-start = ((), (), s32[]{:S(2)}) async-start(), calls=%async_computation.16 | async-start | bytes 4227072 | tf_op jit(solution)/shard_map/reduce_scatter | solution.py:222
  419.9 6.6 copy-start.2
  420.1 1.4 copy-start.4
  423.0 0.7 copy-start.7
  426.5 1322.5 %reduce-scatter.9.cloned.1.call-start = ((), (), s32[]{:S(2)}) async-start(), calls=%async_computation.17 | async-start | bytes 4227072 | tf_op jit(solution)/shard_map/reduce_scatter | solution.py:223
  427.0 0.7 copy-start.8
  427.0 3.6 copy-start.5
  430.5 3.5 copy-start.15
  430.5 1980.2 %reduce-scatter.11.cloned.1.call-start = ((), (), s32[]{:S(2)}) async-start(), calls=%async_computation.18 | async-start | bytes 4227072 | tf_op jit(solution)/shard_map/reduce_scatter | solution.py:224
  431.1 5.6 copy-start.9
  431.1 71.7 %copy-start.22 = (f32[64]{0:T(128)S(1)}, f32[64]{0:T(128)}, u32[]{:S(2)}) copy-start(f32[64]{0:T(128)} %param.28) | copy-start | bytes 772
  434.0 2638.6 %reduce-scatter.13.cloned.1.call-start = ((), (), s32[]{:S(2)}) async-start(), calls=%async_computation.19 | async-start | bytes 4227072 | tf_op jit(solution)/shard_map/reduce_scatter | solution.py:225
  502.8 11.5 copy-start.23
  523.9 13.1 copy-start.10
  526.5 85.3 %all-to-all-start.1 = ((bf16[64,2,4096]{2,1,0:T(2,128)(2,1)}), bf16[64,2,4096]{2,1,0:T(2,128)(2,1)}, u32[]{:S(2)}, u32[]{:S(2)}) async-start(bf16[64,2,4096]{2,1,0:T(2,128)(2,1)} %reshape.327), calls=%async_computation.1 | async-start | bytes 2097152 | tf_op jit(solution)/shard_map/all_to_all | solution.py:132
Sparse Core Ops, SparseCore 0:
  11.1 68.9 all-gather.6
  83.0 62.6 all-gather.8
  148.7 62.6 all-gather.10
  214.3 62.6 all-gather.12
  278.5 19.9 all-gather.14
  300.0 23.8 all-gather.16
  348.4 19.5 reduce-scatter.14
  370.6 20.9 reduce-scatter.16
  426.6 655.7 reduce-scatter.6
  1085.4 663.5 reduce-scatter.8
  1751.9 658.8 reduce-scatter.10
  2413.7 658.8 reduce-scatter.12
where the time goes:
time: 3090 us; the launch traced here: 3080 us
  waiting for transfers between devices  2660 us (86%)
  blocking collectives  203 us (7%)
  matrix products  109 us (4%)
  other arithmetic  36.4 us (1%)
    reduce_scatter x1, waiting for transfers between devices, per_device(): lax.psum_scatter(key_weight_grad, ('rep', 'exp'), scatter_dimension=0, ti...  666 us
    reduce_scatter x1, waiting for transfers between devices, per_device(): lax.psum_scatter(value_weight_grad, ('rep', 'exp'), scatter_dimension=0,...  662 us
    reduce_scatter x1, waiting for transfers between devices, per_device(): lax.psum_scatter(output_weight_grad, ('rep', 'exp'), scatter_dimension=0,...  662 us
    reduce_scatter x1, waiting for transfers between devices, per_device(): lax.psum_scatter(query_weight_grad, ('rep', 'exp'), scatter_dimension=0,...  448 us
    unnamed x2, blocking collectives  137 us
    psum x1, blocking collectives, per_device(): counts = lax.psum(jnp.sum(choose, axis=0).astype(jnp.int32), ('rep', 'exp'))  65.9 us
    all_gather x1, waiting for transfers between devices, per_device(): lax.all_gather(w_key, ('rep', 'exp'), axis=0, tiled=True)  63.4 us
    all_gather x1, waiting for transfers between devices, per_device(): lax.all_gather(w_output, ('rep', 'exp'), axis=0, tiled=True)  62.4 us
  transfers between devices with their start and end apart: 16, of which 10 were waited for; matrix products, arithmetic and copies ran while one was open for 5% of the time, Pallas kernels for 0%

commit v1 on v0

v1 whole, which is shorter than its diff:
```python
import functools

import jax
import jax.numpy as jnp
from jax import lax
from jax.experimental import pallas as pl
from jax.experimental.pallas import tpu as pltpu
from jax.sharding import PartitionSpec as P

HEADS = 16
HEAD_DIM = 64
EPSILON = 1e-05
SWAP = [(0, 1), (1, 0)]
VMEM_LIMIT = 56 * 1024 * 1024


def layer_norm(values, gain, shift):
    center = values - jnp.mean(values, axis=-1, keepdims=True)
    spread = jnp.mean(center * center, axis=-1, keepdims=True)
    return center * lax.rsqrt(spread + EPSILON) * gain + shift


def norm_backward(values, gain, shift, upstream):
    _, norm_pull = jax.vjp(layer_norm, values, gain, shift)
    return norm_pull(upstream)


def swap(value):
    return lax.ppermute(value, "rep", SWAP)


def dot_nt(left, right):
    return lax.dot_general(
        left, right, (((1,), (1,)), ((), ())), preferred_element_type=jnp.float32
    )


def dot_tn(left, right):
    return lax.dot_general(
        left, right, (((0,), (0,)), ((), ())), preferred_element_type=jnp.float32
    )


def params():
    return pltpu.CompilerParams(
        dimension_semantics=("arbitrary",), vmem_limit_bytes=VMEM_LIMIT
    )


def act_grad_kernel(grad_ref, out_w_ref, made_ref):
    made_ref[...] = dot_nt(grad_ref[...], out_w_ref[...]).astype(jnp.bfloat16)


def act_grad_call(grads, weight_out, tile=512):
    rows, width = grads.shape
    hidden = weight_out.shape[0]
    return pl.pallas_call(
        act_grad_kernel,
        grid=(hidden // tile,),
        in_specs=[
            pl.BlockSpec((rows, width), lambda i: (0, 0)),
            pl.BlockSpec((tile, width), lambda i: (i, 0)),
        ],
        out_specs=pl.BlockSpec((rows, tile), lambda i: (0, i)),
        out_shape=jax.ShapeDtypeStruct((rows, hidden), jnp.bfloat16),
        compiler_params=params(),
        cost_estimate=pl.CostEstimate(
            flops=2 * rows * width * hidden, bytes_accessed=10 << 20, transcendentals=0
        ),
        name="act_grad",
    )(grads, weight_out)


def gelu_parts(pre):
    square = pre * pre
    turn = jnp.tanh(0.7978845608028654 * pre * (1.0 + 0.044715 * square))
    half = 0.5 * (1.0 + turn)
    slope = half + 0.5 * pre * (1.0 - turn * turn) * (
        0.7978845608028654 * (1.0 + 3.0 * 0.044715 * square)
    )
    return pre * half, slope


def expert_kernel(rows_ref, in_w_ref, up_ref, act_ref, pre_grad_ref, own_ref, other_ref, total):
    step = pl.program_id(0)
    pre = jnp.dot(rows_ref[...], in_w_ref[...], preferred_element_type=jnp.float32)
    act, slope = gelu_parts(pre)
    act_ref[...] = act.astype(jnp.bfloat16)
    pre_grad = (up_ref[...].astype(jnp.float32) * slope).astype(jnp.bfloat16)
    pre_grad_ref[...] = pre_grad
    made = dot_nt(pre_grad, in_w_ref[...])

    @pl.when(step == 0)
    def _():
        total[...] = made

    @pl.when(step > 0)
    def _():
        total[...] += made

    @pl.when(step == pl.num_programs(0) - 1)
    def _():
        half = own_ref.shape[0]
        own_ref[...] = total[:half, :]
        other_ref[...] = total[half:, :].astype(jnp.bfloat16)


def expert_call(rows_in, weight_in, act_up, tile=256):
    rows, width = rows_in.shape
    hidden = weight_in.shape[1]
    return pl.pallas_call(
        expert_kernel,
        grid=(hidden // tile,),
        in_specs=[
            pl.BlockSpec((rows, width), lambda i: (0, 0)),
            pl.BlockSpec((width, tile), lambda i: (0, i)),
            pl.BlockSpec((rows, tile), lambda i: (0, i)),
        ],
        out_specs=[
            pl.BlockSpec((rows, tile), lambda i: (0, i)),
            pl.BlockSpec((rows, tile), lambda i: (0, i)),
            pl.BlockSpec((rows // 2, width), lambda i: (0, 0)),
            pl.BlockSpec((rows // 2, width), lambda i: (0, 0)),
        ],
        out_shape=[
            jax.ShapeDtypeStruct((rows, hidden), jnp.bfloat16),
            jax.ShapeDtypeStruct((rows, hidden), jnp.bfloat16),
            jax.ShapeDtypeStruct((rows // 2, width), jnp.float32),
            jax.ShapeDtypeStruct((rows // 2, width), jnp.bfloat16),
        ],
        scratch_shapes=[pltpu.VMEM((rows, width), jnp.float32)],
        compiler_params=params(),
        cost_estimate=pl.CostEstimate(
            flops=4 * rows * width * hidden,
            bytes_accessed=24 << 20,
            transcendentals=rows * hidden,
        ),
        name="expert_pre",
    )(rows_in, weight_in, act_up)


def result_kernel(act_ref, out_w_ref, own_ref, other_ref, total):
    step = pl.program_id(0)
    made = jnp.dot(act_ref[...], out_w_ref[...], preferred_element_type=jnp.float32)

    @pl.when(step == 0)
    def _():
        total[...] = made

    @pl.when(step > 0)
    def _():
        total[...] += made

    @pl.when(step == pl.num_programs(0) - 1)
    def _():
        half = own_ref.shape[0]
        own_ref[...] = total[:half, :]
        other_ref[...] = total[half:, :].astype(jnp.bfloat16)


def result_call(act, weight_out, tile=512):
    rows, hidden = act.shape
    width = weight_out.shape[1]
    return pl.pallas_call(
        result_kernel,
        grid=(hidden // tile,),
        in_specs=[
            pl.BlockSpec((rows, tile), lambda i: (0, i)),
            pl.BlockSpec((tile, width), lambda i: (i, 0)),
        ],
        out_specs=[
            pl.BlockSpec((rows // 2, width), lambda i: (0, 0)),
            pl.BlockSpec((rows // 2, width), lambda i: (0, 0)),
        ],
        out_shape=[
            jax.ShapeDtypeStruct((rows // 2, width), jnp.float32),
            jax.ShapeDtypeStruct((rows // 2, width), jnp.bfloat16),
        ],
        scratch_shapes=[pltpu.VMEM((rows, width), jnp.float32)],
        compiler_params=params(),
        cost_estimate=pl.CostEstimate(
            flops=2 * rows * width * hidden, bytes_accessed=12 << 20, transcendentals=0
        ),
        name="expert_result",
    )(act, weight_out)


def weight_grad_kernel(left_ref, right_ref, made_ref):
    made_ref[...] = dot_tn(left_ref[...], right_ref[...])


def weight_grad_call(left, right, split_left, tile=512):
    rows = left.shape[0]
    high, wide = left.shape[1], right.shape[1]
    if split_left:
        grid = high // tile
        left_spec = pl.BlockSpec((rows, tile), lambda i: (0, i))
        right_spec = pl.BlockSpec((rows, wide), lambda i: (0, 0))
        made_spec = pl.BlockSpec((tile, wide), lambda i: (i, 0))
    else:
        grid = wide // tile
        left_spec = pl.BlockSpec((rows, high), lambda i: (0, 0))
        right_spec = pl.BlockSpec((rows, tile), lambda i: (0, i))
        made_spec = pl.BlockSpec((high, tile), lambda i: (0, i))
    return pl.pallas_call(
        weight_grad_kernel,
        grid=(grid,),
        in_specs=[left_spec, right_spec],
        out_specs=made_spec,
        out_shape=jax.ShapeDtypeStruct((high, wide), jnp.float32),
        compiler_params=params(),
        cost_estimate=pl.CostEstimate(
            flops=2 * rows * high * wide, bytes_accessed=14 << 20, transcendentals=0
        ),
        name="weight_grad",
    )(left, right)


def per_device(
    tokens,
    hash_ids,
    doc_lengths,
    w_query,
    w_key,
    w_value,
    w_output,
    norm1_gain,
    norm1_bias,
    norm2_gain,
    norm2_bias,
    expert_in,
    expert_out,
    load_average,
    out_grad,
):
    tok_count, width = tokens.shape
    experts_total = load_average.shape[0]
    groups = lax.axis_size("exp")
    devices = groups * lax.axis_size("rep")
    capacity = 8
    slots = experts_total * capacity
    scale = HEAD_DIM ** (-0.5)
    my_rep = lax.axis_index("rep")
    position = jnp.arange(tok_count, dtype=jnp.int32)

    expert_ids = hash_ids[:, 0]
    choose = (expert_ids[:, None] == jnp.arange(experts_total, dtype=jnp.int32)[None, :]).astype(
        jnp.float32
    )
    own_counts = jnp.sum(choose, axis=0)
    norms = jnp.stack([norm1_gain, norm1_bias, norm2_gain, norm2_bias], axis=1)
    extra = jnp.concatenate(
        [
            norms,
            own_counts.reshape(8, 8).astype(jnp.bfloat16),
            jnp.zeros((8, 116), jnp.bfloat16),
        ],
        axis=1,
    )
    packed = jnp.concatenate([w_query, w_key, w_value, w_output, extra], axis=1)
    gathered = lax.all_gather(packed, ("rep", "exp"), axis=0, tiled=True)

    earlier = (position[None, :] < position[:, None]).astype(jnp.float32)
    before = jnp.dot(earlier, choose, preferred_element_type=jnp.float32)
    rank = jnp.sum(before * choose, axis=1).astype(jnp.int32)
    slot = expert_ids * capacity + rank
    placing = (jnp.arange(slots, dtype=jnp.int32)[:, None] == slot[None, :]).astype(jnp.bfloat16)

    def send_rows(rows):
        outgoing = jnp.dot(placing, rows, preferred_element_type=jnp.float32).astype(jnp.bfloat16)
        outgoing = outgoing.reshape(groups, capacity, width)
        incoming = lax.all_to_all(outgoing, "exp", split_axis=0, concat_axis=0, tiled=True)
        incoming = incoming.reshape(slots, width)
        return jnp.concatenate([incoming, swap(incoming)], axis=0)

    def return_rows(own, other):
        rows = (own + swap(other).astype(jnp.float32)).astype(jnp.bfloat16)
        rows = rows.reshape(groups, capacity, width)
        back = lax.all_to_all(rows, "exp", split_axis=0, concat_axis=0, tiled=True)
        return jnp.einsum(
            "st,sd->td", placing, back.reshape(slots, width), preferred_element_type=jnp.float32
        )

    weight_in, weight_out = expert_in[0], expert_out[0]
    grad_rows = send_rows(out_grad)
    act_up = act_grad_call(grad_rows, weight_out)

    full_qkv = gathered[:, : 3 * width]
    full_output = gathered[:, 3 * width : 4 * width]
    tail = gathered[:, 4 * width :]
    gain_one, bias_one, gain_two, bias_two = (tail[:, i].astype(jnp.float32) for i in range(4))
    counts = (
        jnp.sum(tail[:, 4:12].reshape(devices, 8, 8).astype(jnp.float32), axis=0)
        .reshape(experts_total)
        .astype(jnp.int32)
    )
    new_average = 0.7 * load_average + 0.3 * counts.astype(jnp.float32)

    ends = jnp.cumsum(doc_lengths[0])
    segment = jnp.sum((position[:, None] >= ends[None, :]).astype(jnp.int32), axis=1)
    allowed = (segment[:, None] == segment[None, :]) & (position[None, :] <= position[:, None])
    inputs = tokens.astype(jnp.float32)
    normed_low = layer_norm(inputs, gain_one, bias_one).astype(jnp.bfloat16)
    qkv = jnp.dot(normed_low, full_qkv, preferred_element_type=jnp.float32).astype(jnp.bfloat16)
    queries, keys, values = (
        qkv[:, i * width : (i + 1) * width].reshape(tok_count, HEADS, HEAD_DIM) for i in range(3)
    )
    raw = jnp.einsum("qhd,khd->hqk", queries, keys, preferred_element_type=jnp.float32) * scale
    scores = jnp.where(allowed[None], raw, -1e30)
    top_score = jnp.max(scores, axis=-1, keepdims=True)
    raised = jnp.exp(scores - top_score)
    probs = raised / jnp.sum(raised, axis=-1, keepdims=True)
    probs_low = probs.astype(jnp.bfloat16)
    attended = jnp.einsum("hqk,khd->qhd", probs_low, values, preferred_element_type=jnp.float32)
    attended = attended.astype(jnp.bfloat16).reshape(tok_count, width)
    branch = jnp.dot(attended, full_output, preferred_element_type=jnp.float32)
    hidden_one = inputs + branch
    normed_two_low = layer_norm(hidden_one, gain_two, bias_two).astype(jnp.bfloat16)

    expert_rows = send_rows(normed_two_low)
    act, pre_grad, rows_grad, rows_grad_other = expert_call(expert_rows, weight_in, act_up)
    normed_two_grad = return_rows(rows_grad, rows_grad_other)
    expert_part = return_rows(*result_call(act, weight_out))
    output = (hidden_one + expert_part).astype(jnp.bfloat16)
    in_weight_grad = weight_grad_call(expert_rows, pre_grad, False)[None]
    out_weight_grad = weight_grad_call(act, grad_rows, True)[None]

    upstream = out_grad.astype(jnp.float32)
    hidden_part, gain_two_grad, bias_two_grad = norm_backward(
        hidden_one, gain_two, bias_two, normed_two_grad
    )
    hidden_grad = upstream + hidden_part
    branch_low = hidden_grad.astype(jnp.bfloat16)
    attended_grad = dot_nt(branch_low, full_output)
    attended_grad = attended_grad.astype(jnp.bfloat16).reshape(tok_count, HEADS, HEAD_DIM)
    probs_grad = jnp.einsum(
        "qhd,khd->hqk", attended_grad, values, preferred_element_type=jnp.float32
    )
    value_grad = jnp.einsum(
        "hqk,qhd->khd", probs_low, attended_grad, preferred_element_type=jnp.float32
    ).astype(jnp.bfloat16)
    score_grad = probs * (probs_grad - jnp.sum(probs * probs_grad, axis=-1, keepdims=True))
    score_grad = score_grad.astype(jnp.bfloat16)
    query_grad = (
        jnp.einsum("hqk,khd->qhd", score_grad, keys, preferred_element_type=jnp.float32) * scale
    ).astype(jnp.bfloat16)
    key_grad = (
        jnp.einsum("hqk,qhd->khd", score_grad, queries, preferred_element_type=jnp.float32) * scale
    ).astype(jnp.bfloat16)
    qkv_grad = jnp.concatenate(
        [piece.reshape(tok_count, width) for piece in (query_grad, key_grad, value_grad)], axis=1
    )
    normed_one_grad = dot_nt(qkv_grad, full_qkv)
    input_part, gain_one_grad, bias_one_grad = norm_backward(
        inputs, gain_one, bias_one, normed_one_grad
    )
    input_grad = hidden_grad + input_part

    half = width // 2

    def both(value):
        return jnp.concatenate([value, swap(value)], axis=0)

    def both_halves(value):
        halves = value.reshape(tok_count, 2, half)
        mine = lax.dynamic_index_in_dim(halves, my_rep, 1, keepdims=False)
        theirs = lax.dynamic_index_in_dim(halves, 1 - my_rep, 1, keepdims=False)
        return jnp.concatenate([mine, swap(theirs)], axis=0)

    qkv_weight_grad = dot_tn(both_halves(normed_low), both(qkv_grad))
    output_weight_grad = dot_tn(both_halves(attended), both(branch_low))
    norm_grads = jnp.stack([gain_one_grad, bias_one_grad, gain_two_grad, bias_two_grad], axis=1)
    norm_grads = norm_grads + swap(norm_grads)
    norm_grads = lax.dynamic_slice_in_dim(norm_grads, my_rep * half, half, axis=0)
    partial = jnp.concatenate(
        [
            qkv_weight_grad.astype(jnp.bfloat16),
            output_weight_grad.astype(jnp.bfloat16),
            norm_grads.astype(jnp.bfloat16),
            jnp.zeros((half, 124), jnp.bfloat16),
        ],
        axis=1,
    )
    partial = partial.reshape(groups, 8, 4 * width + 128)
    pieces = lax.all_to_all(partial, "exp", split_axis=0, concat_axis=0, tiled=True)
    summed = jnp.sum(pieces.astype(jnp.float32), axis=0)
    return (
        output,
        input_grad,
        summed[:, :width],
        summed[:, width : 2 * width],
        summed[:, 2 * width : 3 * width],
        summed[:, 3 * width : 4 * width],
        summed[:, 4 * width],
        summed[:, 4 * width + 1],
        summed[:, 4 * width + 2],
        summed[:, 4 * width + 3],
        in_weight_grad,
        out_weight_grad,
        counts,
        new_average,
    )


def solution(mesh):
    rows = P(("rep", "exp"), None)
    vector = P(("rep", "exp"))
    return jax.shard_map(
        per_device,
        mesh=mesh,
        in_specs=(rows,) * 7
        + (vector,) * 4
        + (P("exp", None, "rep"), P("exp", "rep", None), P(), rows),
        out_specs=(rows,) * 6
        + (vector,) * 4
        + (P("exp", None, "rep"), P("exp", "rep", None), P(), P()),
        check_vma=False,
    )
```

time: 3090 us -> 335 us (0.11)
  waiting for transfers between devices: 2660 us -> 126 us
  blocking collectives: 203 us -> 0 us
  matrix products: 109 us -> 34.9 us
  Pallas kernels: 0 us -> 65.7 us
    reduce_scatter x6 -> x0, waiting for transfers between devices: 2440 us -> none  [the longest x1 666 us: per_device(): lax.psum_scatter(key_weight_grad, ('rep', 'exp'), scatter_dimension=0, ti...]
    unnamed x2 -> x0, blocking collectives: 137 us -> none
    all_gather x6 -> x1, waiting for transfers between devices: 186 us -> 64.1 us  [per_device(): gathered = lax.all_gather(packed, ('rep', 'exp'), axis=0, tiled=True)]
    dot_general x24 -> x11, matrix products: 104 us -> 27.7 us  [the longest x2 8.33 us: dot_nt(): lax.dot_general(left, right, (((1,), (1,)), ((), ())), preferred_element_...]
    psum x1 -> x0, blocking collectives: 65.9 us -> none  [per_device(): counts = lax.psum(jnp.sum(choose, axis=0).astype(jnp.int32), ('rep', 'exp'))]
    pallas_call x0 -> x5, Pallas kernels: none -> 65.7 us  [the longest x1 28.8 us: expert_call(): pl.pallas_call(expert_kernel, grid=(hidden // tile,), in_specs=[pl.BlockS...]
  transfers between devices with their start and end apart: 16 -> 15, of which waited for: 10 -> 5; matrix products, arithmetic and copies ran while one was open for 5% -> 21% of each run, Pallas kernels for 0% -> 11%
where the time goes in v1:
time: 335 us; the launch traced here: 330 us
  waiting for transfers between devices  126 us (38%)
  Pallas kernels  65.7 us (20%)
  starting transfers between devices  43.2 us (13%)
  matrix products  34.9 us (10%)
  other arithmetic  25.1 us (7%)
  local copies, waits for them, and re-layouts  20.2 us (6%)
  between operations  14.7 us (4%)
    all_gather x1, waiting for transfers between devices, per_device(): gathered = lax.all_gather(packed, ('rep', 'exp'), axis=0, tiled=True)  64.1 us
    all_to_all x1, waiting for transfers between devices, per_device(): lax.all_to_all(partial, 'exp', split_axis=0, concat_axis=0, tiled=True)  30.5 us
    pallas_call x1, Pallas kernels, expert_call(): pl.pallas_call(expert_kernel, grid=(hidden // tile,), in_specs=[pl.BlockS...  28.8 us
    pallas_call x2, Pallas kernels, weight_grad_call(): pl.pallas_call(weight_grad_kernel, grid=(grid,), in_specs=[left_spec, rig...  18.4 us
    all_to_all x2, starting transfers between devices, send_rows(): lax.all_to_all(outgoing, 'exp', split_axis=0, concat_axis=0, tiled=True)  18.2 us
    all_to_all x2, waiting for transfers between devices, send_rows(): lax.all_to_all(outgoing, 'exp', split_axis=0, concat_axis=0, tiled=True)  17.1 us
    all_to_all x2, waiting for transfers between devices, return_rows(): back = lax.all_to_all(rows, 'exp', split_axis=0, concat_axis=0, tiled=True)  13.6 us
    all_to_all x1, starting transfers between devices, per_device(): lax.all_to_all(partial, 'exp', split_axis=0, concat_axis=0, tiled=True)  10.4 us
  transfers between devices with their start and end apart: 15, of which 5 were waited for; matrix products, arithmetic and copies ran while one was open for 21% of the time, Pallas kernels for 11%

profile of v1, /device:TPU:1, one launch (start us, length us, event | category | flops | bytes accessed | tf_op | source)
XLA Modules:
  0.0 330.2 jit_solution(6870880913571176129)
XLA Ops:
  11.1 1.5 concatenate.27
  12.6 0.9 fusion.33
  14.2 2.3 fusion.21
  16.5 12.0 %all-to-all-start.1 = ((bf16[64,8,1024]{2,1,0:T(8,128)(2,1)}), bf16[64,8,1024]{2,1,0:T(8,128)(2,1)S(1)}, u32[]{:S(2)}, u32[]{:S(2)}) async-start(bf16[64,8,1024]{2,1,0:T(8,128)(2,1)} %fusion.21), calls=%async_computation.1 | async-start | bytes 2097152 | tf_op jit(solution)/shard_map/all_to_all | solution.py:272
  29.3 64.1 %all-gather.2.cloned.1.call-done = bf16[1024,4224]{1,0:T(8,128)(2,1)} async-done(((bf16[8,4224]{1,0:T(8,128)(2,1)}), bf16[1024,4224]{1,0:T(8,128)(2,1)}) %all-gather.2.cloned.1.call-update) | async-done | bytes 8650768 | tf_op jit(solution)/shard_map/all_gather | solution.py:261
  93.4 2.1 convert_reduce_fusion.4
  95.7 3.8 %fusion.5 = bf16[128,3072]{1,0:T(8,128)(2,1)S(1)} fusion(bf16[128,1024]{1,0:T(8,128)(2,1)S(1)} %fusion.46, bf16[1024,4224]{1,0:T(8,128)(2,1)} %all-gather.2.cloned.1.call-done), kind=kOutput, calls=%fused_computation.7 | convolution fusion | flops 805699584 | bytes 7340032 | tf_op jit(solution)/shard_map/dot_general | solution.py:304
  100.1 1.5 fusion.84
  102.3 2.2 fusion.85
  104.9 1.5 fusion.20
  106.4 6.2 %all-to-all-start = ((bf16[64,8,1024]{2,1,0:T(8,128)(2,1)}), bf16[64,8,1024]{2,1,0:T(8,128)(2,1)S(1)}, u32[]{:S(2)}, u32[]{:S(2)}) async-start(bf16[64,8,1024]{2,1,0:T(8,128)(2,1)} %fusion.20), calls=%async_computation | async-start | bytes 2097152 | tf_op jit(solution)/shard_map/all_to_all | solution.py:272
  113.2 17.1 %all-to-all-done = bf16[64,8,1024]{2,1,0:T(8,128)(2,1)S(1)} async-done(((bf16[64,8,1024]{2,1,0:T(8,128)(2,1)}), bf16[64,8,1024]{2,1,0:T(8,128)(2,1)S(1)}, u32[]{:S(2)}, u32[]{:S(2)}) %all-to-all-start) | async-done | bytes 1048608 | tf_op jit(solution)/shard_map/all_to_all | solution.py:272
  130.3 2.0 collective-permute-start
  132.3 2.8 pad_maximum_fusion.1.grad_ref.right_ref
  135.1 8.5 %act_grad.1.up_ref = bf16[1024,2048]{1,0:T(8,128)(2,1)} custom-call(bf16[1024,1024]{1,0:T(8,128)(2,1)} %pad_maximum_fusion.1.grad_ref.right_ref, bf16[2048,1024]{1,0:T(8,128)(2,1)} %bitcast.125), custom_call_target="tpu_custom_call" | custom-call | flops 4294967296 | bytes 10485760 | tf_op jit(solution)/shard_map/act_grad/pallas_call | solution.py:57
  143.5 1.6 pad_maximum_fusion.rows_ref.left_ref
  145.1 28.8 %expert_pre.1 = (bf16[1024,2048]{1,0:T(8,128)(2,1)}, bf16[1024,2048]{1,0:T(8,128)(2,1)}, f32[512,1024]{1,0:T(8,128)}, bf16[512,1024]{1,0:T(8,128)(2,1)}) custom-call(bf16[1024,1024]{1,0:T(8,128)(2,1)} %pad_maximum_fusion.rows_ref.left_ref, bf16[1024,2048]{1,0:T(8,128)(2,1)} %bitcast.124, bf16[1024,2048]{1,0:T(8,128)(2,1)} %act_grad.1.up_ref), custom_call_target="tpu_custom_call" | custom-call | flops 8589934592 | bytes 25165824 | tf_op jit(solution)/shard_map/expert_pre/pallas_call | solution.py:111
  174.0 10.1 %expert_result.1 = (f32[512,1024]{1,0:T(8,128)}, bf16[512,1024]{1,0:T(8,128)(2,1)}) custom-call(bf16[1024,2048]{1,0:T(8,128)(2,1)} %get-tuple-element.20.act_ref.left_ref, bf16[2048,1024]{1,0:T(8,128)(2,1)} %bitcast.126), custom_call_target="tpu_custom_call" | custom-call | flops 4294967296 | bytes 12582912 | tf_op jit(solution)/shard_map/expert_result/pallas_call | solution.py:164
  184.6 1.4 fusion.35
  186.0 4.7 %all-to-all-start.3 = ((bf16[64,8,1024]{2,1,0:T(8,128)(2,1)}), bf16[64,8,1024]{2,1,0:T(8,128)(2,1)S(1)}, u32[]{:S(2)}, u32[]{:S(2)}) async-start(bf16[64,8,1024]{2,1,0:T(8,128)(2,1)} %fusion.35), calls=%async_computation.3 | async-start | bytes 2097152 | tf_op jit(solution)/shard_map/all_to_all | solution.py:279
  190.8 1.6 dynamic-slice_bitcast_fusion.1
  192.5 3.0 fusion.34
  195.5 13.6 %all-to-all-done.3 = bf16[64,8,1024]{2,1,0:T(8,128)(2,1)S(1)} async-done(((bf16[64,8,1024]{2,1,0:T(8,128)(2,1)}), bf16[64,8,1024]{2,1,0:T(8,128)(2,1)S(1)}, u32[]{:S(2)}, u32[]{:S(2)}) %all-to-all-start.3) | async-done | bytes 1048608 | tf_op jit(solution)/shard_map/all_to_all | solution.py:279
  209.1 4.7 %all-to-all-start.2 = ((bf16[64,8,1024]{2,1,0:T(8,128)(2,1)}), bf16[64,8,1024]{2,1,0:T(8,128)(2,1)S(1)}, u32[]{:S(2)}, u32[]{:S(2)}) async-start(bf16[64,8,1024]{2,1,0:T(8,128)(2,1)} %fusion.34), calls=%async_computation.2 | async-start | bytes 2097152 | tf_op jit(solution)/shard_map/all_to_all | solution.py:279
  213.8 1.2 multiply_reduce_fusion.1
  215.7 0.9 fusion.81
  217.5 1.4 collective-permute-start.7
  218.9 3.2 fusion.30
  222.2 1.8 copy.87
  223.9 2.4 convolution_convert_fusion.4
  226.4 1.8 multiply_reduce_fusion
  229.2 0.9 pad_maximum_fusion.2
  230.2 5.1 %fusion.49 = (f32[128]{0:T(128)S(1)}, f32[128,1024]{1,0:T(8,128)S(1)}) fusion(bf16[128,1024]{1,0:T(8,128)(2,1)S(1)} %copy-done, f32[1024]{0:T(1024)S(1)} %get-tuple-element.29, f32[128]{0:T(128)S(1)} %copy-done.23, bf16[1024,4224]{1,0:T(8,128)(2,1)} %all-gather.2.cloned.1.call-done, bf16[128,1024]{0,1:T(8,128)(2,1)S(1)} %bitcast.112, ...), kind=kOutput, calls=%fused_computation.66 | convolution fusion | flops 808320896 | bytes 7869440 | tf_op jit(solution)/shard_map/dot_general | solution.py:33
  235.4 0.9 fusion.47
  236.9 1.7 copy.94
  239.8 1.0 collective-permute-done.8
  240.9 1.0 fusion.54
  241.9 2.5 convolution_convert_fusion.1
  244.4 3.9 %convolution_convert_fusion = bf16[512,3072]{1,0:T(8,128)(2,1)} fusion(bf16[128,3072]{0,1:T(8,128)(2,1)} %collective-permute-done.5, bf16[128,1024]{0,1:T(8,128)(2,1)S(1)} %bitcast.113, bf16[128,1024]{0,1:T(8,128)(2,1)S(1)} %bitcast.101, bf16[128,1024]{0,1:T(8,128)(2,1)S(1)} %bitcast.104, bf16[128,512]{1,0:T(8,128)(2,1)S(1)} %collective-permute-done.4, ...), kind=kOutput, calls=%fused_computation.6 | convolution fusion | flops 813694976 | bytes 4980736 | tf_op jit(solution)/shard_map/dot_general | solution.py:39
  248.3 7.5 %concatenate.35 = bf16[512,4224]{1,0:T(8,128)(2,1)} concatenate(bf16[512,3072]{1,0:T(8,128)(2,1)} %convolution_convert_fusion, bf16[512,1024]{1,0:T(8,128)(2,1)} %convolution_convert_fusion.1, bf16[512,4]{1,0:T(8,128)(2,1)S(1)} %fusion.54, bf16[512,124]{1,0:T(8,128)(2,1)S(1)} %broadcast_in_dim.35), dimensions={1} | concatenate | bytes 8650752 | tf_op jit(solution)/shard_map/concatenate | solution.py:375
  255.8 10.4 %all-to-all-start.4 = ((bf16[64,8,4224]{2,1,0:T(8,128)(2,1)}), bf16[64,8,4224]{2,1,0:T(8,128)(2,1)}, u32[]{:S(2)}, u32[]{:S(2)}) async-start(bf16[64,8,4224]{2,1,0:T(8,128)(2,1)} %bitcast.86), calls=%async_computation.4 | async-start | bytes 8650752 | tf_op jit(solution)/shard_map/all_to_all | solution.py:385
  266.2 1.2 convert_reduce_fusion.2
  268.0 9.2 %weight_grad.3 = f32[2048,1024]{1,0:T(8,128)} custom-call(bf16[1024,2048]{1,0:T(8,128)(2,1)} %get-tuple-element.20.act_ref.left_ref, bf16[1024,1024]{1,0:T(8,128)(2,1)} %pad_maximum_fusion.1.grad_ref.right_ref), custom_call_target="tpu_custom_call" | custom-call | flops 4294967296 | bytes 14680064 | tf_op jit(solution)/shard_map/weight_grad/pallas_call | solution.py:205
  277.2 9.2 %weight_grad.2 = f32[1024,2048]{1,0:T(8,128)} custom-call(bf16[1024,1024]{1,0:T(8,128)(2,1)} %pad_maximum_fusion.rows_ref.left_ref, bf16[1024,2048]{1,0:T(8,128)(2,1)} %get-tuple-element.25.right_ref), custom_call_target="tpu_custom_call" | custom-call | flops 4294967296 | bytes 14680064 | tf_op jit(solution)/shard_map/weight_grad/pallas_call | solution.py:205
  286.5 1.1 fusion.29
  287.5 1.1 add_add_fusion.2
  288.6 30.5 %all-to-all-done.4 = bf16[64,8,4224]{2,1,0:T(8,128)(2,1)} async-done(((bf16[64,8,4224]{2,1,0:T(8,128)(2,1)}), bf16[64,8,4224]{2,1,0:T(8,128)(2,1)}, u32[]{:S(2)}, u32[]{:S(2)}) %all-to-all-start.4) | async-done | bytes 4325408 | tf_op jit(solution)/shard_map/all_to_all | solution.py:385
  319.1 2.8 convert_reduce_fusion
  (142 shorter events, 14.9 us)
Async XLA Ops:
  7.2 21.3 %copy-start.38 = (s32[1,4]{1,0:T(1,128)S(1)}, s32[1,4]{1,0:T(1,128)}, u32[]{:S(2)}) copy-start(s32[1,4]{1,0:T(1,128)} %param.17) | copy-start | bytes 52
  7.2 21.6 %copy-start = (bf16[128,1024]{1,0:T(8,128)(2,1)S(1)}, bf16[128,1024]{1,0:T(8,128)(2,1)}, u32[]{:S(2)}) copy-start(bf16[128,1024]{1,0:T(8,128)(2,1)} %param.15) | copy-start | bytes 786436
  7.2 86.2 %all-gather.2.cloned.1.call-start = ((), (), s32[]{:S(2)}) async-start(), calls=%async_computation.5 | async-start | bytes 8718336 | tf_op jit(solution)/shard_map/all_gather | solution.py:261
  14.2 90.7 %copy-start.20 = (s32[128]{0:T(128)}, s32[128]{0:T(128)S(1)}, u32[]{:S(2)}) copy-start(s32[128]{0:T(128)S(1)} %convert_add_fusion) | copy-start | bytes 1540
  16.5 89.8 %all-to-all-start.1 = ((bf16[64,8,1024]{2,1,0:T(8,128)(2,1)}), bf16[64,8,1024]{2,1,0:T(8,128)(2,1)S(1)}, u32[]{:S(2)}, u32[]{:S(2)}) async-start(bf16[64,8,1024]{2,1,0:T(8,128)(2,1)} %fusion.21), calls=%async_computation.1 | async-start | bytes 2097152 | tf_op jit(solution)/shard_map/all_to_all | solution.py:272
  28.9 70.6 %copy-start.22 = (f32[128]{0:T(128)}, f32[128]{0:T(128)S(1)}, u32[]{:S(2)}) copy-start(f32[128]{0:T(128)S(1)} %broadcast_multiply_fusion.1) | copy-start | bytes 1540
  29.1 70.3 %copy-start.33 = (f32[128]{0:T(128)}, f32[128]{0:T(128)S(1)}, u32[]{:S(2)}) copy-start(f32[128]{0:T(128)S(1)} %fusion.48) | copy-start | bytes 1540
  29.2 70.3 %copy-start.26 = (f32[128]{0:T(128)}, f32[128]{0:T(128)S(1)}, u32[]{:S(2)}) copy-start(f32[128]{0:T(128)S(1)} %fusion.73) | copy-start | bytes 1540
  29.3 72.3 %copy-start.16 = (pred[128,128]{0,1:T(8,128)(4,1)}, pred[128,128]{0,1:T(8,128)(4,1)S(1)}, u32[]{:S(2)}) copy-start(pred[128,128]{0,1:T(8,128)(4,1)S(1)} %fusion.71) | copy-start | bytes 49156
  99.7 2.6 copy-start.4
  101.6 3.0 copy-start.18
  102.3 4.0 %copy-start.12 = (bf16[16,64,128]{2,1,0:T(8,128)(2,1)}, bf16[16,64,128]{2,1,0:T(8,128)(2,1)S(1)}, u32[]{:S(2)}) copy-start(bf16[16,64,128]{2,1,0:T(8,128)(2,1)S(1)} %convolution_convert_fusion.5) | copy-start | bytes 786436
  104.6 30.4 %copy-start.17 = (f32[128]{0:T(128)}, f32[128]{0:T(128)S(1)}, u32[]{:S(2)}) copy-start(f32[128]{0:T(128)S(1)} %broadcast_multiply_fusion) | copy-start | bytes 1540
  104.8 30.2 %copy-start.37 = (f32[128]{0:T(128)}, f32[128]{0:T(128)S(1)}, u32[]{:S(2)}) copy-start(f32[128]{0:T(128)S(1)} %multiply_reduce_fusion.3) | copy-start | bytes 1540
  104.8 30.2 %copy-start.25 = (f32[128]{0:T(128)}, f32[128]{0:T(128)S(1)}, u32[]{:S(2)}) copy-start(f32[128]{0:T(128)S(1)} %fusion.74) | copy-start | bytes 1540
  106.4 23.9 %all-to-all-start = ((bf16[64,8,1024]{2,1,0:T(8,128)(2,1)}), bf16[64,8,1024]{2,1,0:T(8,128)(2,1)S(1)}, u32[]{:S(2)}, u32[]{:S(2)}) async-start(bf16[64,8,1024]{2,1,0:T(8,128)(2,1)} %fusion.20), calls=%async_computation | async-start | bytes 2097152 | tf_op jit(solution)/shard_map/all_to_all | solution.py:272
  112.6 19.7 %collective-permute-start.1 = (bf16[512,1024]{1,0:T(8,128)(2,1)S(1)}, bf16[512,1024]{1,0:T(8,128)(2,1)}, u32[]{:S(2)}, u32[]{:S(2)}) collective-permute-start(bf16[512,1024]{1,0:T(8,128)(2,1)S(1)} %bitcast.87), channel_id=1, source_target_pairs={{0,64},{64,0},{1,65},{65,1},{2,66},{66,2},{3,67},{67,3},{4,68},{68... | collective-permute-start | bytes 3145736 | tf_op jit(solution)/shard_map/ppermute | solution.py:29
  130.3 13.3 %collective-permute-start = (bf16[512,1024]{1,0:T(8,128)(2,1)S(1)}, bf16[512,1024]{1,0:T(8,128)(2,1)S(1)}, u32[]{:S(2)}, u32[]{:S(2)}) collective-permute-start(bf16[512,1024]{1,0:T(8,128)(2,1)S(1)} %bitcast.89), channel_id=1, source_target_pairs={{0,64},{64,0},{1,65},{65,1},{2,66},{66,2},{3,67},{67,3},{4,68},{68... | collective-permute-start | bytes 3145736 | tf_op jit(solution)/shard_map/ppermute | solution.py:29
  173.9 10.7 %collective-permute-start.3 = (bf16[512,1024]{1,0:T(8,128)(2,1)}, bf16[512,1024]{1,0:T(8,128)(2,1)S(1)}, u32[]{:S(2)}, u32[]{:S(2)}) collective-permute-start(bf16[512,1024]{1,0:T(8,128)(2,1)} %get-tuple-element.24), channel_id=1, source_target_pairs={{0,64},{64,0},{1,65},{65,1},{2,66},{66,2},{3,67},{67,3},{4,68},{68... | collective-permute-start | bytes 3145736 | tf_op jit(solution)/shard_map/ppermute | solution.py:29
  174.0 10.6 %copy-start.2 = (f32[512,1024]{1,0:T(8,128)S(1)}, f32[512,1024]{1,0:T(8,128)}, u32[]{:S(2)}) copy-start(f32[512,1024]{1,0:T(8,128)} %get-tuple-element.23) | copy-start | bytes 6291460
  184.1 8.4 %collective-permute-start.2 = (bf16[512,1024]{1,0:T(8,128)(2,1)}, bf16[512,1024]{1,0:T(8,128)(2,1)S(1)}, u32[]{:S(2)}, u32[]{:S(2)}) collective-permute-start(bf16[512,1024]{1,0:T(8,128)(2,1)} %get-tuple-element.22), channel_id=1, source_target_pairs={{0,64},{64,0},{1,65},{65,1},{2,66},{66,2},{3,67},{67,3},{4,68},{68... | collective-permute-start | bytes 3145736 | tf_op jit(solution)/shard_map/ppermute | solution.py:29
  186.0 23.1 %all-to-all-start.3 = ((bf16[64,8,1024]{2,1,0:T(8,128)(2,1)}), bf16[64,8,1024]{2,1,0:T(8,128)(2,1)S(1)}, u32[]{:S(2)}, u32[]{:S(2)}) async-start(bf16[64,8,1024]{2,1,0:T(8,128)(2,1)} %fusion.35), calls=%async_computation.3 | async-start | bytes 2097152 | tf_op jit(solution)/shard_map/all_to_all | solution.py:279
  192.5 49.4 %collective-permute-start.6 = (bf16[128,512]{0,1:T(8,128)(2,1)}, bf16[128,512]{0,1:T(8,128)(2,1)}, u32[]{:S(2)}, u32[]{:S(2)}) collective-permute-start(bf16[128,512]{0,1:T(8,128)(2,1)} %get-tuple-element.46), channel_id=1, source_target_pairs={{0,64},{64,0},{1,65},{65,1},{2,66},{66,2},{3,67},{67,3},{4,68},{68... | collective-permute-start | bytes 393224 | tf_op jit(solution)/shard_map/ppermute | solution.py:29
  195.5 21.2 %copy-start.1 = (bf16[128,1024]{1,0:T(8,128)(2,1)S(1)}, bf16[128,1024]{1,0:T(8,128)(2,1)}, u32[]{:S(2)}) copy-start(bf16[128,1024]{1,0:T(8,128)(2,1)} %param.29) | copy-start | bytes 786436
  209.1 46.7 %all-to-all-start.2 = ((bf16[64,8,1024]{2,1,0:T(8,128)(2,1)}), bf16[64,8,1024]{2,1,0:T(8,128)(2,1)S(1)}, u32[]{:S(2)}, u32[]{:S(2)}) async-start(bf16[64,8,1024]{2,1,0:T(8,128)(2,1)} %fusion.34), calls=%async_computation.2 | async-start | bytes 2097152 | tf_op jit(solution)/shard_map/all_to_all | solution.py:279
  215.0 9.0 %copy-start.5 = (bf16[128,1024]{0,1:T(8,128)(2,1)S(1)}, bf16[128,1024]{0,1:T(8,128)(2,1)}, u32[]{:S(2)}) copy-start(bf16[128,1024]{0,1:T(8,128)(2,1)} %copy-done.4) | copy-start | bytes 786436
  215.0 9.0 %copy-start.7 = (bf16[128,1024]{0,1:T(8,128)(2,1)S(1)}, bf16[128,1024]{0,1:T(8,128)(2,1)}, u32[]{:S(2)}) copy-start(bf16[128,1024]{0,1:T(8,128)(2,1)} %copy-done.6) | copy-start | bytes 786436
  216.7 9.7 %copy-start.29 = (f32[128]{0:T(128)}, f32[128]{0:T(128)S(1)}, u32[]{:S(2)}) copy-start(f32[128]{0:T(128)S(1)} %negate_multiply_fusion.1) | copy-start | bytes 1540
  217.5 24.3 %collective-permute-start.7 = (bf16[128,1024]{1,0:T(8,128)(2,1)}, bf16[128,1024]{1,0:T(8,128)(2,1)}, u32[]{:S(2)}, u32[]{:S(2)}) collective-permute-start(bf16[128,1024]{1,0:T(8,128)(2,1)} %fusion.53), channel_id=1, source_target_pairs={{0,64},{64,0},{1,65},{65,1},{2,66},{66,2},{3,67},{67,3},{4,68},{68... | collective-permute-start | bytes 786440 | tf_op jit(solution)/shard_map/ppermute | solution.py:29
  228.9 6.4 %copy-start.8 = (bf16[16,64,128]{2,1,0:T(8,128)(2,1)}, bf16[16,64,128]{2,1,0:T(8,128)(2,1)S(1)}, u32[]{:S(2)}) copy-start(bf16[16,64,128]{2,1,0:T(8,128)(2,1)S(1)} %fusion.28) | copy-start | bytes 786436
  229.2 6.1 %copy-start.10 = (bf16[16,64,128]{2,1,0:T(8,128)(2,1)}, bf16[16,64,128]{2,1,0:T(8,128)(2,1)S(1)}, u32[]{:S(2)}) copy-start(bf16[16,64,128]{2,1,0:T(8,128)(2,1)S(1)} %fusion.27) | copy-start | bytes 786436
  230.2 5.1 %copy-start.34 = (f32[128]{0:T(128)S(1)}, f32[128]{0:T(128)}, u32[]{:S(2)}) copy-start(f32[128]{0:T(128)} %copy-done.33) | copy-start | bytes 1540
  230.2 5.2 %copy-start.27 = (f32[128]{0:T(128)S(1)}, f32[128]{0:T(128)}, u32[]{:S(2)}) copy-start(f32[128]{0:T(128)} %copy-done.26) | copy-start | bytes 1540
  230.2 14.2 %collective-permute-start.5 = (bf16[128,3072]{0,1:T(8,128)(2,1)}, bf16[128,3072]{0,1:T(8,128)(2,1)}, u32[]{:S(2)}, u32[]{:S(2)}) collective-permute-start(bf16[128,3072]{0,1:T(8,128)(2,1)} %pad_maximum_fusion.2), channel_id=1, source_target_pairs={{0,64},{64,0},{1,65},{65,1},{2,66},{66,2},{3,67},{67,3},{4,68},{68... | collective-permute-start | bytes 2359304 | tf_op jit(solution)/shard_map/ppermute | solution.py:29
  238.6 5.8 %copy-start.9 = (bf16[16,64,128]{2,1,0:T(8,128)(2,1)S(1)}, bf16[16,64,128]{2,1,0:T(8,128)(2,1)}, u32[]{:S(2)}) copy-start(bf16[16,64,128]{2,1,0:T(8,128)(2,1)} %copy-done.8) | copy-start | bytes 786436
  238.6 5.8 %copy-start.11 = (bf16[16,64,128]{2,1,0:T(8,128)(2,1)S(1)}, bf16[16,64,128]{2,1,0:T(8,128)(2,1)}, u32[]{:S(2)}) copy-start(bf16[16,64,128]{2,1,0:T(8,128)(2,1)} %copy-done.10) | copy-start | bytes 786436
  238.6 5.8 %copy-start.15 = (bf16[16,64,128]{2,1,0:T(8,128)(2,1)S(1)}, bf16[16,64,128]{2,1,0:T(8,128)(2,1)}, u32[]{:S(2)}) copy-start(bf16[16,64,128]{2,1,0:T(8,128)(2,1)} %convolution_convert_fusion.4) | copy-start | bytes 786436
  238.6 2.2 collective-permute-start.8
  239.7 4.7 %collective-permute-start.4 = (bf16[128,512]{1,0:T(8,128)(2,1)S(1)}, bf16[128,512]{1,0:T(8,128)(2,1)S(1)}, u32[]{:S(2)}, u32[]{:S(2)}) collective-permute-start(bf16[128,512]{1,0:T(8,128)(2,1)S(1)} %bitcast.115), channel_id=1, source_target_pairs={{0,64},{64,0},{1,65},{65,1},{2,66},{66,2},{3,67},{67,3},{4,68},{68... | collective-permute-start | bytes 393224 | tf_op jit(solution)/shard_map/ppermute | solution.py:29
  255.8 11.7 %copy-start.39 = (f32[64]{0:T(128)S(1)}, f32[64]{0:T(128)}, u32[]{:S(2)}) copy-start(f32[64]{0:T(128)} %param.28) | copy-start | bytes 772
  255.8 63.3 %all-to-all-start.4 = ((bf16[64,8,4224]{2,1,0:T(8,128)(2,1)}), bf16[64,8,4224]{2,1,0:T(8,128)(2,1)}, u32[]{:S(2)}, u32[]{:S(2)}) async-start(bf16[64,8,4224]{2,1,0:T(8,128)(2,1)} %bitcast.86), calls=%async_computation.4 | async-start | bytes 8650752 | tf_op jit(solution)/shard_map/all_to_all | solution.py:385
  267.5 9.7 %copy-start.36 = (s32[64]{0:T(128)}, s32[64]{0:T(128)S(1)}, u32[]{:S(2)}) copy-start(s32[64]{0:T(128)S(1)} %convert_element_type.204) | copy-start | bytes 772
  277.2 9.3 %copy-start.35 = (f32[128]{0:T(128)S(1)}, f32[128]{0:T(128)}, u32[]{:S(2)}) copy-start(f32[128]{0:T(128)} %get-tuple-element.33) | copy-start | bytes 1540
  277.2 9.3 %copy-start.21 = (s32[128]{0:T(128)S(1)}, s32[128]{0:T(128)}, u32[]{:S(2)}) copy-start(s32[128]{0:T(128)} %copy-done.20) | copy-start | bytes 1540
  277.2 10.4 %copy-start.24 = (f32[128]{0:T(128)S(1)}, f32[128]{0:T(128)}, u32[]{:S(2)}) copy-start(f32[128]{0:T(128)} %copy-done.22) | copy-start | bytes 1540
  277.2 10.3 %copy-start.28 = (f32[128]{0:T(128)S(1)}, f32[128]{0:T(128)}, u32[]{:S(2)}) copy-start(f32[128]{0:T(128)} %copy-done.26) | copy-start | bytes 1540
  277.2 10.3 %copy-start.30 = (f32[128]{0:T(128)S(1)}, f32[128]{0:T(128)}, u32[]{:S(2)}) copy-start(f32[128]{0:T(128)} %copy-done.29) | copy-start | bytes 1540
  277.2 10.3 %copy-start.32 = (f32[128]{0:T(128)S(1)}, f32[128]{0:T(128)}, u32[]{:S(2)}) copy-start(f32[128]{0:T(128)} %copy-done.31) | copy-start | bytes 1540
  (7 other events, 12.2 us)
Sparse Core Ops, SparseCore 0:
  12.7 80.5 all-gather.1
